TPU v7x, 512 devices: a whole 4x4x16 slice. The times are simulated.
512 devices in a mesh: clus: 16 (over z_lo, x), dir: 32 (over y, z_hi, core).
Axes of the slice: x: 4, y: 4, z: 16 (z_hi: 4, z_lo: 4; z = z_hi * 4 + z_lo), core: 2. Of those that a mesh axis runs over, the one named last changes fastest.
Arguments:
- child_patterns: float32 [768, 2, 256, 128], P('clus', None, 'dir'), may hold values from -6 to 6
- trans_table: bfloat16 [316, 2, 73728], P(None, None, 'dir'), may hold values from -0.875 to 0.875
- child_parent: int32 [16, 48], P('clus'), may hold values from 0 to 7, never falling along the last dimension, each value on 1 to 8 neighbouring positions
- child_octant: int32 [768], P('clus'), may hold values from 0 to 7
- partner_src: int32 [128, 56], replicated, may hold values from 0 to 127, as said below
- partner_off: int32 [128, 56], replicated, may hold values from 0 to 315
- partner_count: int32 [128], replicated, may hold values from 15 to 56, as said below
Outputs:
- child_incoming: float32 [768, 2, 256, 128], P('clus', None, 'dir')
Inputs may be any that keep to these rules, and one draw needn't show every extreme that they name: `partner_src`: each row lists 56 distinct parent clusters, none equal to the row's own index. `partner_count`: the number of live slots at the head of each row of partner_src and partner_off. On one index of clus, all of its 8 parents have 56 live slots. `child_parent`: Non-decreasing along each row; every one of the 8 parents of the row has 1 to 8 children.
All inputs are finite; a program needn't handle non-finite values.
Results may differ from a plain program's by a relative error of at most 0.0003.
Values sent between devices are 32-bit elements; how exact they have to be, the bound alone decides.
A program may use at most 64 MiB of HBM per device.

v0:
```python
import math
import jax
import jax.numpy as jnp
from jax import lax
from jax.sharding import PartitionSpec as P

NTHETA_C = 128
NPHI_C = 256
NTHETA_P = 192
NPHI_P = 384
phase_scale = 8.0 * math.pi
highest = lax.Precision.HIGHEST


def with_halo(shard, sides, width):
    for axis, dim in sides:
        size, length = (lax.axis_size(axis), shard.shape[dim])
        up = [(i, (i + 1) % size) for i in range(size)]
        down = [(j, i) for i, j in up]
        last = lax.slice_in_dim(shard, length - width, length, axis=dim)
        initial = lax.slice_in_dim(shard, 0, width, axis=dim)
        before = lax.ppermute(last, axis, up)
        after = lax.ppermute(initial, axis, down)
        shard = jnp.concatenate([before, shard, after], axis=dim)
    return shard


def lagrange(offset):
    weights = []
    for anchor in range(5):
        factor = jnp.ones_like(offset)
        for neighbour in range(5):
            if neighbour != anchor:
                factor = factor * (offset - neighbour) / (anchor - neighbour)
        weights.append(factor)
    return weights


def polar_matrix_of(rows_out, rows_in):
    target = (jnp.arange(rows_out, dtype=jnp.float32) + 0.5) * rows_in / rows_out - 0.5
    start_row = jnp.clip(jnp.floor(target + 0.5).astype(jnp.int32) - 2, 0, rows_in - 5)
    weights = lagrange(target - start_row.astype(jnp.float32))
    columns = jnp.arange(rows_in, dtype=jnp.int32)
    matrix = jnp.zeros((rows_out, rows_in), jnp.float32)
    for anchor in range(5):
        matrix = matrix + jnp.where(
            columns[None, :] == (start_row + anchor)[:, None], weights[anchor][:, None], 0.0
        )
    return matrix


def azimuth_matrix_of(out_index, in_index, total_out, total_in):
    target = (out_index * total_in).astype(jnp.float32) / total_out
    nearest = jnp.floor(target + 0.5).astype(jnp.int32)
    weights = lagrange(target - nearest.astype(jnp.float32) + 2.0)
    matrix = jnp.zeros((out_index.shape[0], in_index.shape[0]), jnp.float32)
    for anchor in range(5):
        columns = nearest + anchor - 2
        matrix = matrix + jnp.where(
            in_index[None, :] == columns[:, None], weights[anchor][:, None], 0.0
        )
    return matrix


def shift_phases(octant, azimuth_index, azimuth_total, polar_total):
    azimuth = 2.0 * math.pi * azimuth_index.astype(jnp.float32) / azimuth_total
    polar = math.pi * (jnp.arange(polar_total, dtype=jnp.float32) + 0.5) / polar_total
    first_axis = jnp.sin(polar)[None, :] * jnp.cos(azimuth)[:, None]
    second_axis = jnp.sin(polar)[None, :] * jnp.sin(azimuth)[:, None]
    third_axis = jnp.cos(polar)[None, :] * jnp.ones_like(azimuth)[:, None]
    first_sign = (1 - 2 * (octant % 2)).astype(jnp.float32)
    second_sign = (1 - 2 * (octant // 2 % 2)).astype(jnp.float32)
    third_sign = (1 - 2 * (octant // 4)).astype(jnp.float32)
    phase_angle = phase_scale * (
        first_sign[:, None, None] * first_axis[None]
        + second_sign[:, None, None] * second_axis[None]
        + third_sign[:, None, None] * third_axis[None]
    )
    return (jnp.cos(phase_angle), jnp.sin(phase_angle))


def translate(sources, table, partner_src, partner_off, partner_count):
    live_mask = (
        jnp.arange(partner_src.shape[1], dtype=jnp.int32)[None, :] < partner_count[:, None]
    ).astype(jnp.float32)
    picked = sources[partner_src]
    operator = table[partner_off].astype(jnp.float32) * live_mask[:, :, None, None]
    real_part = jnp.sum(
        operator[:, :, 0] * picked[:, :, 0] - operator[:, :, 1] * picked[:, :, 1], axis=1
    )
    imaginary = jnp.sum(
        operator[:, :, 0] * picked[:, :, 1] + operator[:, :, 1] * picked[:, :, 0], axis=1
    )
    return jnp.stack([real_part, imaginary], axis=1)


def forward_shift(patterns, cosine, sine_part):
    real_part = patterns[:, 0] * cosine - patterns[:, 1] * sine_part
    imaginary = patterns[:, 0] * sine_part + patterns[:, 1] * cosine
    return jnp.stack([real_part, imaginary], axis=1)


def conjugate_shift(patterns, cosine, sine_part):
    real_part = patterns[:, 0] * cosine + patterns[:, 1] * sine_part
    imaginary = patterns[:, 1] * cosine - patterns[:, 0] * sine_part
    return jnp.stack([real_part, imaginary], axis=1)


def on_device(
    child_patterns, trans_table, child_parent, child_octant, partner_src, partner_off, partner_count
):
    child_slots, _, azimuth_in, polar_in = child_patterns.shape
    polar_out = NTHETA_P
    azimuth_out = trans_table.shape[2] // polar_out
    parent_slots = partner_src.shape[0] // lax.axis_size("clus")
    cluster_index = lax.axis_index("clus")
    direction_index = lax.axis_index("dir")
    parents = child_parent[0]
    polar_matrix = polar_matrix_of(NTHETA_P, NTHETA_C)
    onehot = (parents[None, :] == jnp.arange(parent_slots, dtype=jnp.int32)[:, None]).astype(
        jnp.float32
    )
    own_rows = jnp.mod(
        direction_index * azimuth_out + jnp.arange(azimuth_out, dtype=jnp.int32), NPHI_P
    )
    cosine, sine_part = shift_phases(child_octant, own_rows, NPHI_P, polar_out)
    extended = with_halo(child_patterns, (("dir", 2),), 2)
    gather_matrix = azimuth_matrix_of(
        jnp.arange(azimuth_out, dtype=jnp.int32),
        jnp.arange(azimuth_in + 4, dtype=jnp.int32) - 2,
        NPHI_P,
        NPHI_C,
    )
    along_azimuth = jnp.einsum("pc,kacz->kapz", gather_matrix, extended, precision=highest)
    refined = jnp.einsum("kapz,tz->kapt", along_azimuth, polar_matrix, precision=highest)
    shifted = forward_shift(refined, cosine, sine_part)
    radiation = jnp.einsum("gk,kapt->gapt", onehot, shifted, precision=highest)
    flattened = radiation.reshape(parent_slots, 2, azimuth_out * polar_out)
    sources = lax.all_gather(flattened, "clus", axis=0, tiled=True)
    first_row = cluster_index * parent_slots
    own_src = lax.dynamic_slice_in_dim(partner_src, first_row, parent_slots, 0)
    own_off = lax.dynamic_slice_in_dim(partner_off, first_row, parent_slots, 0)
    own_count = lax.dynamic_slice_in_dim(partner_count, first_row, parent_slots, 0)
    incoming = translate(sources, trans_table, own_src, own_off, own_count)
    incoming = incoming.reshape(parent_slots, 2, azimuth_out, polar_out)
    return_matrix = azimuth_matrix_of(
        jnp.arange(azimuth_out + 6, dtype=jnp.int32) - 3,
        jnp.arange(azimuth_in, dtype=jnp.int32),
        NPHI_P,
        NPHI_C,
    )
    per_child = jnp.einsum("gk,gapt->kapt", onehot, incoming, precision=highest)
    returned = conjugate_shift(per_child, cosine, sine_part)
    coarse_own = jnp.einsum("kapt,tz->kapz", returned, polar_matrix, precision=highest)
    coarse = with_halo(coarse_own, (("dir", 2),), 3)
    return jnp.einsum("pc,kapz->kacz", return_matrix, coarse, precision=highest)


def solution(mesh):
    return jax.shard_map(
        on_device,
        mesh=mesh,
        in_specs=(
            P("clus", None, "dir", None),
            P(None, None, "dir"),
            P("clus", None),
            P("clus"),
            P(),
            P(),
            P(),
        ),
        out_specs=P("clus", None, "dir", None),
        check_vma=False,
    )
```

profile of v0, /device:TPU:1, one launch (start us, length us, event | category | flops | bytes accessed | tf_op | source)
XLA Modules:
  0.0 204.3 jit_solution(9964516812942284886)
XLA Ops:
  6.5 0.0 copy-start
  6.5 0.0 all-gather.2.cloned.1.call-start
  6.5 1.3 fusion.124
  7.9 0.0 copy-start.4
  7.9 0.0 copy-start.1
  7.9 0.0 copy-start.2
  7.9 10.3 %collective-permute-start = (f32[48,2,2,128]{3,2,1,0:T(2,128)S(1)}, f32[48,2,2,128]{3,2,1,0:T(2,128)S(1)}, u32[]{:S(2)}, u32[]{:S(2)}) collective-permute-start(f32[48,2,2,128]{3,2,1,0:T(2,128)S(1)} %get-tuple-element.13), channel_id=1, source_target_pairs={{0,1},{1,2},{2,3},{3,4},{4,5},{5,6},{6,7},{7,8},{8,9},{9,10},{10,1... | collective-permute-start | bytes 294920 | tf_op jit(solution)/shard_map/ppermute | solution.py:22
  18.3 1.9 collective-permute-start.1
  20.5 0.1 fusion.113
  20.6 0.7 fusion.106
  21.2 0.1 broadcast_multiply_fusion.1
  21.3 0.0 collective-permute-done
  21.3 6.8 %collective-permute-done.1 = f32[48,2,2,128]{3,2,1,0:T(2,128)S(1)} collective-permute-done((f32[48,2,2,128]{3,2,1,0:T(2,128)S(1)}, f32[48,2,2,128]{3,2,1,0:T(2,128)S(1)}, u32[]{:S(2)}, u32[]{:S(2)}) %collective-permute-start.1) | collective-permute-done | bytes 98336 | tf_op jit(solution)/shard_map/ppermute | solution.py:23
  28.1 2.0 convolution_bitcast_fusion
  30.1 1.5 fusion.14
  31.7 2.6 %multiply_subtract_fusion.1 = (f32[48,1,12,192]{3,0,2,1:T(8,128)S(1)}, f32[48,1,12,192]{3,0,2,1:T(8,128)S(1)}) fusion(f32[48,2,12,192]{3,0,2,1:T(8,128)S(1)} %fusion.14, f32[192]{0:T(256)S(1)} %fusion.102, f32[48]{0:T(128)S(1)} %get-tuple-element.19, f32[12,192]{1,0:T(8,128)S(1)} %get-tuple-element.16, f32[48]{0:T(128)S(1)} %get-tuple-element.18, ...), kind=kLoop, calls=%fused_computation.27 | loop fusion | flops 1327104 | bytes 1789248 | tf_op jit(solution)/shard_map/sub | solution.py:98
  34.3 0.0 copy-done.3
  34.3 0.5 fusion
  34.8 0.1 copy.36
  34.9 0.8 reshape.383
  35.7 0.0 all-gather.2.cloned.1.call-update
  35.8 0.0 copy-done.4
  35.8 0.1 dynamic_slice.10
  35.8 0.1 compare_select_fusion
  35.9 0.1 copy.28
  36.0 0.1 reshape.368
  36.1 0.1 copy.24
  36.1 0.1 reshape.360
  36.2 0.0 copy-done
  36.3 20.4 %gather_fusion = bf16[448,2,2304]{2,1,0:T(2,128)(2,1)} fusion(bf16[316,2,2304]{2,1,0:T(2,128)(2,1)S(1)} %copy-done, s32[1024]{0:T(1024)S(1)} %pad_clamp_fusion.1), kind=kCustom, calls=%fused_computation | custom fusion | bytes 8259328 | tf_op jit(solution)/shard_map/gather | solution.py:87
  56.7 0.1 fusion.86
  56.8 8.4 %convert_multiply_fusion = f32[8,56,2,2304]{3,2,1,0:T(2,128)} fusion(bf16[8,56,2,2304]{3,2,1,0:T(2,128)(2,1)} %bitcast.32, f32[8,56]{1,0:T(8,128)S(1)} %fusion.86), kind=kLoop, calls=%fused_computation.2 | loop fusion | flops 4128768 | bytes 12388096 | tf_op jit(solution)/shard_map/mul | solution.py:87
  65.2 53.1 %all-gather.2.cloned.1.call-done = f32[128,2,2304]{2,1,0:T(2,128)} async-done(((f32[8,2,2304]{2,1,0:T(2,128)}), f32[128,2,2304]{2,1,0:T(2,128)}) %all-gather.2.cloned.1.call-update) | async-done | bytes 2359312 | tf_op jit(solution)/shard_map/all_gather | solution.py:139
  118.2 22.7 %gather_fusion.1 = f32[448,2,2304]{2,1,0:T(2,128)} fusion(f32[128,2,2304]{2,1,0:T(2,128)} %all-gather.2.cloned.1.call-done, s32[1024]{0:T(1024)S(1)} %pad_clamp_fusion), kind=kCustom, calls=%fused_computation.1 | custom fusion | bytes 16516864 | tf_op jit(solution)/shard_map/gather | solution.py:86
  140.9 22.2 %subtract_reduce_fusion = (f32[8,2304]{1,0:T(8,128)S(1)}, f32[8,2304]{1,0:T(8,128)S(1)}) fusion(f32[8,56,2,2304]{3,2,1,0:T(2,128)} %bitcast.31, f32[8,56,2,2304]{3,2,1,0:T(2,128)} %convert_multiply_fusion), kind=kLoop, calls=%fused_computation.4 | loop fusion | flops 8220672 | bytes 16662528 | tf_op jit(solution)/shard_map/reduce_sum | solution.py:88
  163.2 0.1 stack.20
  163.2 0.1 copy.29
  163.3 0.1 stack.21
  163.4 0.1 copy.30
  163.5 0.7 fusion.18
  164.1 2.4 %multiply_add_fusion = (f32[48,1,12,192]{3,0,2,1:T(8,128)S(1)}, f32[48,1,12,192]{3,0,2,1:T(8,128)S(1)}) fusion(f32[48,2,12,192]{3,0,2,1:T(8,128)S(1)} %fusion.18, f32[192]{0:T(256)S(1)} %fusion.102, f32[48]{0:T(128)S(1)} %get-tuple-element.19, f32[12,192]{1,0:T(8,128)S(1)} %get-tuple-element.16, f32[48]{0:T(128)S(1)} %get-tuple-element.18, ...), kind=kLoop, calls=%fused_computation.25 | loop fusion | flops 1327104 | bytes 1789248 | tf_op jit(solution)/shard_map/add | solution.py:104
  166.6 1.4 fusion.4
  168.0 16.7 %collective-permute-start.2 = (f32[48,2,3,128]{3,0,2,1:T(8,128)S(1)}, f32[48,2,3,128]{3,0,2,1:T(8,128)S(1)}, u32[]{:S(2)}, u32[]{:S(2)}) collective-permute-start(f32[48,2,3,128]{3,0,2,1:T(8,128)S(1)} %get-tuple-element.11), channel_id=1, source_target_pairs={{0,1},{1,2},{2,3},{3,4},{4,5},{5,6},{6,7},{7,8},{8,9},{9,10},{10,1... | collective-permute-start | bytes 442376 | tf_op jit(solution)/shard_map/ppermute | solution.py:22
  184.7 1.9 collective-permute-start.3
  186.7 0.1 collective-permute-done.2
  186.8 8.8 %collective-permute-done.3 = f32[48,2,3,128]{3,0,2,1:T(8,128)S(1)} collective-permute-done((f32[48,2,3,128]{3,0,2,1:T(8,128)S(1)}, f32[48,2,3,128]{3,0,2,1:T(8,128)S(1)}, u32[]{:S(2)}, u32[]{:S(2)}) %collective-permute-start.3) | collective-permute-done | bytes 147488 | tf_op jit(solution)/shard_map/ppermute | solution.py:23
  195.6 0.1 pad_maximum_fusion
  195.6 1.8 convolution_bitcast_fusion.1
  (25 shorter events, 0.4 us)
Async XLA Ops:
  6.5 29.7 %copy-start = (bf16[316,2,2304]{2,1,0:T(2,128)(2,1)S(1)}, bf16[316,2,2304]{2,1,0:T(2,128)(2,1)}, u32[]{:S(2)}) copy-start(bf16[316,2,2304]{2,1,0:T(2,128)(2,1)} %param.8) | copy-start | bytes 8736772
  6.5 27.7 %copy-start.3 = (s32[1,48]{1,0:T(1,128)S(1)}, s32[1,48]{1,0:T(1,128)}, u32[]{:S(2)}) copy-start(s32[1,48]{1,0:T(1,128)} %param.9) | copy-start | bytes 580
  6.5 111.7 %all-gather.2.cloned.1.call-start = ((), (), s32[]{:S(2)}) async-start(), calls=%async_computation | async-start | bytes 2506752 | tf_op jit(solution)/shard_map/all_gather | solution.py:139
  7.9 27.9 %copy-start.4 = (s32[128]{0:T(128)S(1)}, s32[128]{0:T(128)}, u32[]{:S(2)}) copy-start(s32[128]{0:T(128)} %param.13) | copy-start | bytes 1540
  7.9 27.9 %copy-start.1 = (s32[128,56]{0,1:T(8,128)S(1)}, s32[128,56]{0,1:T(8,128)}, u32[]{:S(2)}) copy-start(s32[128,56]{0,1:T(8,128)} %param.11) | copy-start | bytes 86020
  7.9 27.9 %copy-start.2 = (s32[128,56]{0,1:T(8,128)S(1)}, s32[128,56]{0,1:T(8,128)}, u32[]{:S(2)}) copy-start(s32[128,56]{0,1:T(8,128)} %param.12) | copy-start | bytes 86020
  7.9 13.4 %collective-permute-start = (f32[48,2,2,128]{3,2,1,0:T(2,128)S(1)}, f32[48,2,2,128]{3,2,1,0:T(2,128)S(1)}, u32[]{:S(2)}, u32[]{:S(2)}) collective-permute-start(f32[48,2,2,128]{3,2,1,0:T(2,128)S(1)} %get-tuple-element.13), channel_id=1, source_target_pairs={{0,1},{1,2},{2,3},{3,4},{4,5},{5,6},{6,7},{7,8},{8,9},{9,10},{10,1... | collective-permute-start | bytes 294920 | tf_op jit(solution)/shard_map/ppermute | solution.py:22
  18.3 9.9 %collective-permute-start.1 = (f32[48,2,2,128]{3,2,1,0:T(2,128)S(1)}, f32[48,2,2,128]{3,2,1,0:T(2,128)S(1)}, u32[]{:S(2)}, u32[]{:S(2)}) collective-permute-start(f32[48,2,2,128]{3,2,1,0:T(2,128)S(1)} %get-tuple-element.14), channel_id=1, source_target_pairs={{1,0},{2,1},{3,2},{4,3},{5,4},{6,5},{7,6},{8,7},{9,8},{10,9},{11,1... | collective-permute-start | bytes 294920 | tf_op jit(solution)/shard_map/ppermute | solution.py:23
  168.0 18.8 %collective-permute-start.2 = (f32[48,2,3,128]{3,0,2,1:T(8,128)S(1)}, f32[48,2,3,128]{3,0,2,1:T(8,128)S(1)}, u32[]{:S(2)}, u32[]{:S(2)}) collective-permute-start(f32[48,2,3,128]{3,0,2,1:T(8,128)S(1)} %get-tuple-element.11), channel_id=1, source_target_pairs={{0,1},{1,2},{2,3},{3,4},{4,5},{5,6},{6,7},{7,8},{8,9},{9,10},{10,1... | collective-permute-start | bytes 442376 | tf_op jit(solution)/shard_map/ppermute | solution.py:22
  184.7 10.8 %collective-permute-start.3 = (f32[48,2,3,128]{3,0,2,1:T(8,128)S(1)}, f32[48,2,3,128]{3,0,2,1:T(8,128)S(1)}, u32[]{:S(2)}, u32[]{:S(2)}) collective-permute-start(f32[48,2,3,128]{3,0,2,1:T(8,128)S(1)} %get-tuple-element.12), channel_id=1, source_target_pairs={{1,0},{2,1},{3,2},{4,3},{5,4},{6,5},{7,6},{8,7},{9,8},{10,9},{11,1... | collective-permute-start | bytes 442376 | tf_op jit(solution)/shard_map/ppermute | solution.py:23
Sparse Core Ops, SparseCore 0:
  35.9 82.3 all-gather.1
where the time goes:
time: 205 us; the launch traced here: 204 us
  waiting for transfers between devices  68.7 us (34%)
  local copies, waits for them, and re-layouts  46 us (22%)
  other arithmetic  37.1 us (18%)
  starting transfers between devices  30.9 us (15%)
  between operations  13.6 us (7%)
  matrix products  7.9 us (4%)
    all_gather x1, waiting for transfers between devices, on_device(): sources = lax.all_gather(flattened, 'clus', axis=0, tiled=True)  53.1 us
    ppermute x2, starting transfers between devices, with_halo(): before = lax.ppermute(last, axis, up)  27 us
    gather x1, local copies, waits for them, and re-layouts, translate(): picked = sources[partner_src]  22.7 us
    reduce_sum x1, other arithmetic, translate(): jnp.sum(operator[:, :, 0] * picked[:, :, 0] - operator[:, :, 1] * picked[...  22.2 us
    gather x1, local copies, waits for them, and re-layouts, translate(): table[partner_off].astype(jnp.float32) * live_mask[:, :, None, None]  20.4 us
    ppermute x2, waiting for transfers between devices, with_halo(): after = lax.ppermute(initial, axis, down)  15.5 us
    mul x1, other arithmetic, translate(): table[partner_off].astype(jnp.float32) * live_mask[:, :, None, None]  8.36 us
  transfers between devices with their start and end apart: 5, of which 4 were waited for; matrix products, arithmetic and copies ran while one was open for 15% of the time, Pallas kernels for 0%

commit v1 on v0

--- a/solution.py
+++ b/solution.py
@@ -136,7 +136,9 @@
     shifted = forward_shift(refined, cosine, sine_part)
     radiation = jnp.einsum("gk,kapt->gapt", onehot, shifted, precision=highest)
     flattened = radiation.reshape(parent_slots, 2, azimuth_out * polar_out)
-    sources = lax.all_gather(flattened, "clus", axis=0, tiled=True)
+    sources = jnp.concatenate(
+        lax.all_to_all(jnp.stack([flattened] * lax.axis_size("clus")), "clus", 0, 0), axis=0
+    )
     first_row = cluster_index * parent_slots
     own_src = lax.dynamic_slice_in_dim(partner_src, first_row, parent_slots, 0)
     own_off = lax.dynamic_slice_in_dim(partner_off, first_row, parent_slots, 0)

time: 205 us -> 159 us (0.78)
  the two profiles are of different devices: /device:TPU:1 before, /device:TPU:37 now
where the time goes in v1:
time: 159 us
  local copies, waits for them, and re-layouts  47.7 us (30%)
  waiting for transfers between devices  42.7 us (27%)
  other arithmetic  36.8 us (23%)
  starting transfers between devices  23.6 us (15%)
  matrix products  7.9 us (5%)
    all_to_all x1, waiting for transfers between devices, on_device(): lax.all_to_all(jnp.stack([flattened] * lax.axis_size('clus')), 'clus', 0, 0)  24.5 us
    gather x1, local copies, waits for them, and re-layouts, translate(): picked = sources[partner_src]  22.7 us
    reduce_sum x1, other arithmetic, translate(): jnp.sum(operator[:, :, 0] * picked[:, :, 0] - operator[:, :, 1] * picked[...  22.2 us
    gather x1, local copies, waits for them, and re-layouts, translate(): table[partner_off].astype(jnp.float32) * live_mask[:, :, None, None]  20.4 us
    ppermute x2, waiting for transfers between devices, with_halo(): after = lax.ppermute(initial, axis, down)  15.9 us
    ppermute x2, starting transfers between devices, with_halo(): before = lax.ppermute(last, axis, up)  11.5 us
    mul x1, other arithmetic, translate(): table[partner_off].astype(jnp.float32) * live_mask[:, :, None, None]  8.35 us
    all_to_all x1, starting transfers between devices, on_device(): lax.all_to_all(jnp.stack([flattened] * lax.axis_size('clus')), 'clus', 0, 0)  7.71 us
  transfers between devices with their start and end apart: 5, of which 5 were waited for; matrix products, arithmetic and copies ran while one was open for 19% of the time, Pallas kernels for 0%

profile of v1, /device:TPU:37, one launch (start us, length us, event | category | flops | bytes accessed | tf_op | source)
XLA Modules:
  0.0 158.9 jit_solution(4985036024523522615)
XLA Ops:
  0.0 0.0 copy-start
  0.0 1.3 fusion.126
  1.4 9.4 %collective-permute-start = (f32[48,2,2,128]{3,2,1,0:T(2,128)S(1)}, f32[48,2,2,128]{3,2,1,0:T(2,128)S(1)}, u32[]{:S(2)}, u32[]{:S(2)}) collective-permute-start(f32[48,2,2,128]{3,2,1,0:T(2,128)S(1)} %get-tuple-element.13), channel_id=1, source_target_pairs={{0,1},{1,2},{2,3},{3,4},{4,5},{5,6},{6,7},{7,8},{8,9},{9,10},{10,1... | collective-permute-start | bytes 294920 | tf_op jit(solution)/shard_map/ppermute | solution.py:22
  10.7 1.9 %collective-permute-start.1 = (f32[48,2,2,128]{3,2,1,0:T(2,128)S(1)}, f32[48,2,2,128]{3,2,1,0:T(2,128)S(1)}, u32[]{:S(2)}, u32[]{:S(2)}) collective-permute-start(f32[48,2,2,128]{3,2,1,0:T(2,128)S(1)} %get-tuple-element.14), channel_id=1, source_target_pairs={{1,0},{2,1},{3,2},{4,3},{5,4},{6,5},{7,6},{8,7},{9,8},{10,9},{11,1... | collective-permute-start | bytes 294920 | tf_op jit(solution)/shard_map/ppermute | solution.py:23
  13.0 0.1 fusion.115
  13.0 0.7 fusion.108
  13.7 0.1 broadcast_multiply_fusion.1
  13.8 0.2 collective-permute-done
  14.0 6.8 %collective-permute-done.1 = f32[48,2,2,128]{3,2,1,0:T(2,128)S(1)} collective-permute-done((f32[48,2,2,128]{3,2,1,0:T(2,128)S(1)}, f32[48,2,2,128]{3,2,1,0:T(2,128)S(1)}, u32[]{:S(2)}, u32[]{:S(2)}) %collective-permute-start.1) | collective-permute-done | bytes 98336 | tf_op jit(solution)/shard_map/ppermute | solution.py:23
  20.7 2.0 %fusion.9 = f32[48,2,128,12]{2,3,1,0:T(8,128)S(1)} fusion(f32[48,2,2,128]{3,2,1,0:T(2,128)S(1)} %collective-permute-done.1, f32[48,2,8,128]{3,2,1,0:T(8,128)} %param.7, f32[48,2,2,128]{3,2,1,0:T(2,128)S(1)} %collective-permute-done, f32[12]{0:T(128)S(1)} %get-tuple-element.20, f32[12]{0:T(128)S(1)} %get-tuple-element.21, f32[12]{0:T(128)S(1)} %get-tuple-element.22, ...), kind=kOutput, calls=%fused_computation.16 | convolution fusion | flops 21530592 | bytes 1180176 | tf_op jit(solution)/shard_map/pc,kacz->kapz/dot_general | solution.py:134
  22.8 1.5 fusion.15
  24.3 2.4 %multiply_subtract_fusion.1 = (f32[48,1,12,192]{3,0,2,1:T(8,128)S(1)}, f32[48,1,12,192]{3,0,2,1:T(8,128)S(1)}) fusion(f32[48,2,12,192]{3,0,2,1:T(8,128)S(1)} %fusion.15, f32[192]{0:T(256)S(1)} %fusion.104, f32[48]{0:T(128)S(1)} %get-tuple-element.19, f32[12,192]{1,0:T(8,128)S(1)} %get-tuple-element.16, f32[48]{0:T(128)S(1)} %get-tuple-element.18, ...), kind=kLoop, calls=%fused_computation.28 | loop fusion | flops 1327104 | bytes 1789248 | tf_op jit(solution)/shard_map/sub | solution.py:98
  26.7 0.0 copy-done.3
  26.7 0.5 fusion
  27.2 0.0 copy-start.4
  27.3 0.0 copy-start.1
  27.3 0.0 copy-start.2
  27.3 0.1 copy.21
  27.4 0.2 reshape.385
  27.5 2.3 %stack.23 = f32[16,8,2,2304]{3,2,1,0:T(2,128)} broadcast(f32[8,2,2304]{2,1,0:T(2,128)S(1)} %reshape.385), dimensions={1,2,3} | broadcast | bytes 2506752 | tf_op jit(solution)/shard_map/stack | solution.py:140
  29.8 7.7 %all-to-all-start = ((f32[16,8,2,2304]{3,2,1,0:T(2,128)}), f32[16,8,2,2304]{3,2,1,0:T(2,128)}, u32[]{:S(2)}, u32[]{:S(2)}) async-start(f32[16,8,2,2304]{3,2,1,0:T(2,128)} %stack.23), calls=%async_computation | async-start | bytes 4718592 | tf_op jit(solution)/shard_map/all_to_all | solution.py:140
  37.5 0.0 copy-done.4
  37.5 0.1 dynamic_slice.10
  37.6 0.1 compare_select_fusion
  37.7 0.1 copy.12
  37.8 0.1 reshape.370
  37.9 0.1 copy.9
  37.9 0.1 reshape.362
  38.0 0.0 copy-done
  38.0 20.4 %gather_fusion = bf16[448,2,2304]{2,1,0:T(2,128)(2,1)} fusion(bf16[316,2,2304]{2,1,0:T(2,128)(2,1)S(1)} %copy-done, s32[1024]{0:T(1024)S(1)} %pad_clamp_fusion.1), kind=kCustom, calls=%fused_computation | custom fusion | bytes 8259328 | tf_op jit(solution)/shard_map/gather | solution.py:87
  58.5 0.1 fusion.88
  58.6 8.4 %convert_multiply_fusion = f32[8,56,2,2304]{3,2,1,0:T(2,128)} fusion(bf16[8,56,2,2304]{3,2,1,0:T(2,128)(2,1)} %bitcast.34, f32[8,56]{1,0:T(8,128)S(1)} %fusion.88), kind=kLoop, calls=%fused_computation.2 | loop fusion | flops 4128768 | bytes 12388096 | tf_op jit(solution)/shard_map/mul | solution.py:87
  67.0 24.5 %all-to-all-done = f32[16,8,2,2304]{3,2,1,0:T(2,128)} async-done(((f32[16,8,2,2304]{3,2,1,0:T(2,128)}), f32[16,8,2,2304]{3,2,1,0:T(2,128)}, u32[]{:S(2)}, u32[]{:S(2)}) %all-to-all-start) | async-done | bytes 2359328 | tf_op jit(solution)/shard_map/all_to_all | solution.py:140
  91.5 22.7 %gather_fusion.1 = f32[448,2,2304]{2,1,0:T(2,128)} fusion(f32[128,2,2304]{2,1,0:T(2,128)} %bitcast.10, s32[1024]{0:T(1024)S(1)} %pad_clamp_fusion), kind=kCustom, calls=%fused_computation.1 | custom fusion | bytes 16516864 | tf_op jit(solution)/shard_map/gather | solution.py:86
  114.2 22.2 %subtract_reduce_fusion = (f32[8,2304]{1,0:T(8,128)S(1)}, f32[8,2304]{1,0:T(8,128)S(1)}) fusion(f32[8,56,2,2304]{3,2,1,0:T(2,128)} %bitcast.33, f32[8,56,2,2304]{3,2,1,0:T(2,128)} %convert_multiply_fusion), kind=kLoop, calls=%fused_computation.4 | loop fusion | flops 8220672 | bytes 16662528 | tf_op jit(solution)/shard_map/reduce_sum | solution.py:88
  136.3 0.1 stack.24
  136.4 0.1 copy.13
  136.5 0.1 stack.25
  136.6 0.1 copy.14
  136.6 0.7 fusion.20
  137.3 2.4 %multiply_add_fusion = (f32[48,1,12,192]{3,0,2,1:T(8,128)S(1)}, f32[48,1,12,192]{3,0,2,1:T(8,128)S(1)}) fusion(f32[48,2,12,192]{3,0,2,1:T(8,128)S(1)} %fusion.20, f32[192]{0:T(256)S(1)} %fusion.104, f32[48]{0:T(128)S(1)} %get-tuple-element.19, f32[12,192]{1,0:T(8,128)S(1)} %get-tuple-element.16, f32[48]{0:T(128)S(1)} %get-tuple-element.18, ...), kind=kLoop, calls=%fused_computation.26 | loop fusion | flops 1327104 | bytes 1789248 | tf_op jit(solution)/shard_map/add | solution.py:104
  139.8 1.4 fusion.4
  141.2 2.1 %collective-permute-start.2 = (f32[48,2,3,128]{3,0,2,1:T(8,128)S(1)}, f32[48,2,3,128]{3,0,2,1:T(8,128)S(1)}, u32[]{:S(2)}, u32[]{:S(2)}) collective-permute-start(f32[48,2,3,128]{3,0,2,1:T(8,128)S(1)} %get-tuple-element.11), channel_id=1, source_target_pairs={{0,1},{1,2},{2,3},{3,4},{4,5},{5,6},{6,7},{7,8},{8,9},{9,10},{10,1... | collective-permute-start | bytes 442376 | tf_op jit(solution)/shard_map/ppermute | solution.py:22
  143.3 2.4 %collective-permute-start.3 = (f32[48,2,3,128]{3,0,2,1:T(8,128)S(1)}, f32[48,2,3,128]{3,0,2,1:T(8,128)S(1)}, u32[]{:S(2)}, u32[]{:S(2)}) collective-permute-start(f32[48,2,3,128]{3,0,2,1:T(8,128)S(1)} %get-tuple-element.12), channel_id=1, source_target_pairs={{1,0},{2,1},{3,2},{4,3},{5,4},{6,5},{7,6},{8,7},{9,8},{10,9},{11,1... | collective-permute-start | bytes 442376 | tf_op jit(solution)/shard_map/ppermute | solution.py:23
  145.8 2.1 %collective-permute-done.2 = f32[48,2,3,128]{3,0,2,1:T(8,128)S(1)} collective-permute-done((f32[48,2,3,128]{3,0,2,1:T(8,128)S(1)}, f32[48,2,3,128]{3,0,2,1:T(8,128)S(1)}, u32[]{:S(2)}, u32[]{:S(2)}) %collective-permute-start.2) | collective-permute-done | bytes 147488 | tf_op jit(solution)/shard_map/ppermute | solution.py:22
  147.9 9.1 %collective-permute-done.3 = f32[48,2,3,128]{3,0,2,1:T(8,128)S(1)} collective-permute-done((f32[48,2,3,128]{3,0,2,1:T(8,128)S(1)}, f32[48,2,3,128]{3,0,2,1:T(8,128)S(1)}, u32[]{:S(2)}, u32[]{:S(2)}) %collective-permute-start.3) | collective-permute-done | bytes 147488 | tf_op jit(solution)/shard_map/ppermute | solution.py:23
  157.0 0.1 pad_maximum_fusion
  157.1 1.8 %convolution_bitcast_fusion = f32[48,2,8,128]{3,2,1,0:T(8,128)} fusion(f32[48,2,18,128]{3,0,2,1:T(8,128)S(1)} %pad_maximum_fusion, f32[18]{0:T(128)S(1)} %get-tuple-element.42, s32[18]{0:T(128)S(1)} %get-tuple-element.48, f32[18]{0:T(128)S(1)} %get-tuple-element.43, s32[18]{0:T(128)S(1)} %get-tuple-element.49, f32[18]{0:T(128)S(1)} %get-tuple-element.44, ...), kind=kOutput, calls=%fused_computation.5 | convolution fusion | flops 21235680 | bytes 1278672 | tf_op jit(solution)/shard_map/pc,kapz->kacz/dot_general | solution.py:158
  (25 shorter events, 0.4 us)
Async XLA Ops:
  0.0 38.0 %copy-start = (bf16[316,2,2304]{2,1,0:T(2,128)(2,1)S(1)}, bf16[316,2,2304]{2,1,0:T(2,128)(2,1)}, u32[]{:S(2)}) copy-start(bf16[316,2,2304]{2,1,0:T(2,128)(2,1)} %param.8) | copy-start | bytes 8736772
  0.0 26.7 %copy-start.3 = (s32[1,48]{1,0:T(1,128)S(1)}, s32[1,48]{1,0:T(1,128)}, u32[]{:S(2)}) copy-start(s32[1,48]{1,0:T(1,128)} %param.9) | copy-start | bytes 580
  1.4 12.6 %collective-permute-start = (f32[48,2,2,128]{3,2,1,0:T(2,128)S(1)}, f32[48,2,2,128]{3,2,1,0:T(2,128)S(1)}, u32[]{:S(2)}, u32[]{:S(2)}) collective-permute-start(f32[48,2,2,128]{3,2,1,0:T(2,128)S(1)} %get-tuple-element.13), channel_id=1, source_target_pairs={{0,1},{1,2},{2,3},{3,4},{4,5},{5,6},{6,7},{7,8},{8,9},{9,10},{10,1... | collective-permute-start | bytes 294920 | tf_op jit(solution)/shard_map/ppermute | solution.py:22
  10.7 10.0 %collective-permute-start.1 = (f32[48,2,2,128]{3,2,1,0:T(2,128)S(1)}, f32[48,2,2,128]{3,2,1,0:T(2,128)S(1)}, u32[]{:S(2)}, u32[]{:S(2)}) collective-permute-start(f32[48,2,2,128]{3,2,1,0:T(2,128)S(1)} %get-tuple-element.14), channel_id=1, source_target_pairs={{1,0},{2,1},{3,2},{4,3},{5,4},{6,5},{7,6},{8,7},{9,8},{10,9},{11,1... | collective-permute-start | bytes 294920 | tf_op jit(solution)/shard_map/ppermute | solution.py:23
  27.2 10.3 %copy-start.4 = (s32[128]{0:T(128)S(1)}, s32[128]{0:T(128)}, u32[]{:S(2)}) copy-start(s32[128]{0:T(128)} %param.13) | copy-start | bytes 1540
  27.3 10.4 %copy-start.1 = (s32[128,56]{0,1:T(8,128)S(1)}, s32[128,56]{0,1:T(8,128)}, u32[]{:S(2)}) copy-start(s32[128,56]{0,1:T(8,128)} %param.11) | copy-start | bytes 86020
  27.3 10.4 %copy-start.2 = (s32[128,56]{0,1:T(8,128)S(1)}, s32[128,56]{0,1:T(8,128)}, u32[]{:S(2)}) copy-start(s32[128,56]{0,1:T(8,128)} %param.12) | copy-start | bytes 86020
  29.8 61.6 %all-to-all-start = ((f32[16,8,2,2304]{3,2,1,0:T(2,128)}), f32[16,8,2,2304]{3,2,1,0:T(2,128)}, u32[]{:S(2)}, u32[]{:S(2)}) async-start(f32[16,8,2,2304]{3,2,1,0:T(2,128)} %stack.23), calls=%async_computation | async-start | bytes 4718592 | tf_op jit(solution)/shard_map/all_to_all | solution.py:140
  141.2 6.7 %collective-permute-start.2 = (f32[48,2,3,128]{3,0,2,1:T(8,128)S(1)}, f32[48,2,3,128]{3,0,2,1:T(8,128)S(1)}, u32[]{:S(2)}, u32[]{:S(2)}) collective-permute-start(f32[48,2,3,128]{3,0,2,1:T(8,128)S(1)} %get-tuple-element.11), channel_id=1, source_target_pairs={{0,1},{1,2},{2,3},{3,4},{4,5},{5,6},{6,7},{7,8},{8,9},{9,10},{10,1... | collective-permute-start | bytes 442376 | tf_op jit(solution)/shard_map/ppermute | solution.py:22
  143.3 13.7 %collective-permute-start.3 = (f32[48,2,3,128]{3,0,2,1:T(8,128)S(1)}, f32[48,2,3,128]{3,0,2,1:T(8,128)S(1)}, u32[]{:S(2)}, u32[]{:S(2)}) collective-permute-start(f32[48,2,3,128]{3,0,2,1:T(8,128)S(1)} %get-tuple-element.12), channel_id=1, source_target_pairs={{1,0},{2,1},{3,2},{4,3},{5,4},{6,5},{7,6},{8,7},{9,8},{10,9},{11,1... | collective-permute-start | bytes 442376 | tf_op jit(solution)/shard_map/ppermute | solution.py:23
